TPU v7x, 32 devices: a whole 2x2x4 slice. The times are simulated.
32 devices in a mesh: rows: 16 (over z, y, core), rep: 2 (over x).
Axes of the slice: x: 2, y: 2, z: 4, core: 2. Of those that a mesh axis runs over, the one named last changes fastest.
Arguments:
- embeddings: bfloat16 [11264, 1024], P(('rows', 'rep')), may hold values from -6 to 6
- owner_ids: int32 [11264, 1], P(('rows', 'rep')), may hold values from 0 to 15; in each aligned block of 352 rows (0 to 351, 352 to 703, ...) at most 64 rows name the same one
- live_mask: int32 [11264], P(('rows', 'rep')), may hold values 0 or 1
Outputs:
- neighbour_means: bfloat16 [11264, 1024], P(('rows', 'rep'))
Inputs may be any that keep to these rules, and one draw needn't show every extreme that they name: `owner_ids`: among the rows of one device, at most 64 name the same owner, and in every draw some owner is named by exactly 64 of them.
All inputs are finite; a program needn't handle non-finite values. Where the computation divides by a largest or mean magnitude, that divisor is 1e-20 or more. No bound on the sum of `live_mask` on one device may be relied on, other than what follows from the above.
Results may differ from a plain program's by a relative error of at most 0.0017.
The roundings to bfloat16 on the way count: a program that leaves them out, or rounds other values in their place, can miss the bound.
Values may be sent and summed in bfloat16 or wider, within the bound.
A program may use at most 64 MiB of HBM per device.

v0:
```python
import jax
import jax.numpy as jnp
from jax import lax
from jax.sharding import PartitionSpec as P

BUCKET = 1024
JOIN_ROWS = 8192
KERNEL_SCALE = 4.0
EPSILON = 1e-06
SPLIT = lax.Precision.HIGH
PRECISE = lax.Precision.HIGHEST


def block_positions(owner_block, owners, slot_cap):
    rows = owner_block.shape[0]
    same = owner_block[:, None] == owner_block[None, :]
    index = jnp.arange(rows, dtype=jnp.int32)
    earlier = index[None, :] < index[:, None]
    slot_rank = jnp.sum((same & earlier).astype(jnp.int32), axis=1)
    return owner_block * slot_cap + slot_rank


def whiten(embedded, inverse_root):
    mapped = jnp.dot(embedded, inverse_root, preferred_element_type=jnp.float32)
    return (mapped * lax.rsqrt(jnp.mean(mapped * mapped, axis=1, keepdims=True) + EPSILON)).astype(
        jnp.bfloat16
    )


def root_of(moment):
    y = moment / jnp.max(jnp.sum(jnp.abs(moment), axis=1))
    eye = jnp.eye(y.shape[0], dtype=jnp.float32)
    square = jnp.dot(y, y, precision=SPLIT)
    inner = 1.6875 * eye - 0.5625 * y + 0.0625 * square
    return (2.25 * eye - 2.4375 * y + jnp.dot(square, inner, precision=SPLIT)).astype(jnp.bfloat16)


def masked_means(queries, members, same, alive):
    scores = lax.dot_general(
        queries, members, (((1,), (1,)), ((), ())), preferred_element_type=jnp.float32
    )
    weights = jnp.where(same, jnp.exp(KERNEL_SCALE * (scores / members.shape[1] - 1.0)), 0.0)
    denominator = jnp.sum(weights, axis=1, keepdims=True)
    summed = jnp.dot(weights.astype(jnp.bfloat16), members, preferred_element_type=jnp.float32)
    averaged = summed / jnp.where(alive[:, None] > 0, denominator, 1.0)
    normed = averaged * lax.rsqrt(jnp.mean(averaged * averaged, axis=1, keepdims=True) + EPSILON)
    return (normed * alive[:, None]).astype(jnp.bfloat16)


def spread(values, positions, slots_all):
    return jnp.zeros((slots_all,) + values.shape[1:], values.dtype).at[positions].set(values)


def by_exchange(embeddings, owner_ids, live_mask):
    rows_here, columns = embeddings.shape
    owners = lax.axis_size("rows")
    slot_cap = BUCKET // owners
    positions = block_positions(owner_ids[:, 0], owners, slot_cap)
    live_rows = live_mask.astype(jnp.bfloat16)
    masked = embeddings * live_rows[:, None]
    partial_moment = lax.dot_general(
        masked, masked, (((0,), (0,)), ((), ())), preferred_element_type=jnp.float32
    )
    inverse_root = root_of(lax.psum(partial_moment, ("rows", "rep")))
    whitened = whiten(embeddings, inverse_root)

    def swapped(values):
        return lax.all_to_all(values, "rows", split_axis=0, concat_axis=0, tiled=True)

    members = swapped(
        spread(whitened, positions, BUCKET).reshape(owners, slot_cap, columns)
    ).reshape(BUCKET, columns)
    alive = swapped(spread(live_rows, positions, BUCKET).reshape(owners, slot_cap))
    alive = alive.reshape(BUCKET).astype(jnp.float32)
    means = masked_means(members, members, alive[None, :] > 0, alive)
    returned = swapped(means.reshape(owners, slot_cap, columns))
    return returned.reshape(BUCKET, columns)[positions]


def by_gather(embeddings, owner_ids, live_mask):
    rows_here, columns = embeddings.shape
    owners = lax.axis_size("rows")
    key = jnp.where(live_mask > 0, owner_ids[:, 0], -1)
    keys = lax.all_gather(key, "rows", axis=0, tiled=True)
    everyone = lax.all_gather(embeddings, "rows", axis=0, tiled=True)
    share = columns // owners
    masked = everyone * (keys >= 0).astype(jnp.bfloat16)[:, None]
    own = lax.dynamic_slice_in_dim(masked, lax.axis_index("rows") * share, share, 1)
    part = lax.dot_general(
        own, masked, (((0,), (0,)), ((), ())), preferred_element_type=jnp.float32
    )
    part = lax.psum(part, "rep")
    moment = lax.all_gather(part, "rows", axis=0, tiled=True)
    whitened = whiten(everyone, root_of(moment))
    mine = lax.dynamic_slice_in_dim(whitened, lax.axis_index("rows") * rows_here, rows_here, 0)
    alive = (live_mask > 0).astype(jnp.float32)
    return masked_means(mine, whitened, owner_ids == keys[None, :], alive)


def solution(mesh):
    placed = (P(("rows", "rep"), None), P(("rows", "rep"), None), P(("rows", "rep")))

    def per_device(embeddings, owner_ids, live_mask):
        gathered = embeddings.shape[0] * mesh.shape["rows"]
        join = by_gather if gathered <= JOIN_ROWS else by_exchange
        return join(embeddings, owner_ids, live_mask)

    return jax.shard_map(
        per_device, mesh=mesh, in_specs=placed, out_specs=P(("rows", "rep"), None), check_vma=False
    )
```

profile of v0, /device:TPU:0, one launch (start us, length us, event | category | flops | bytes accessed | tf_op | source)
XLA Modules:
  0.0 265.8 jit_solution(3059865663002023440)
XLA Ops:
  6.5 0.7 all-gather.3.cloned.1.call-update
  7.3 0.0 all-reduce.3.cloned.1.call-start
  7.3 0.7 reduce.1
  8.0 1.2 dynamic-slice.4
  9.9 0.7 fusion.31
  10.6 0.1 select_dynamic-update-slice_fusion
  10.7 65.3 %all-reduce = s32[5632]{0:T(1024)S(1)} all-reduce(s32[5632]{0:T(1024)S(1)} %select_dynamic-update-slice_fusion), channel_id=1, replica_groups=mesh['rows'=16,'rep'=2] {'rows'}, use_global_device_ids=true, to_apply=%add | all-reduce | flops 5632 | bytes 45056
  76.0 31.2 %all-gather.3.cloned.1.call-done = bf16[5632,1024]{1,0:T(8,128)(2,1)} async-done(((bf16[352,1024]{1,0:T(8,128)(2,1)}), bf16[5632,1024]{1,0:T(8,128)(2,1)}) %all-gather.3.cloned.1.call-update) | async-done | bytes 11534352 | tf_op jit(solution)/shard_map/all_gather | solution.py:85
  107.2 7.0 %broadcast_multiply_fusion = bf16[5632,1024]{1,0:T(8,128)(2,1)S(1)} fusion(bf16[5632,1024]{1,0:T(8,128)(2,1)} %all-gather.3.cloned.1.call-done, bf16[5632]{0:T(1024)(128)(2,1)S(1)} %compare_convert_fusion), kind=kLoop, calls=%fused_computation.7 | loop fusion | flops 5767168 | bytes 23079936 | tf_op jit(solution)/shard_map/mul | solution.py:87
  114.2 3.3 %fusion.19 = f32[64,1024]{1,0:T(8,128)} fusion(bf16[5632,1024]{1,0:T(8,128)(2,1)S(1)} %broadcast_multiply_fusion, s32[]{:T(128)S(6)} %select_n.20), kind=kOutput, calls=%fused_computation.27 | convolution fusion | flops 738197504 | bytes 13238276 | tf_op jit(solution)/shard_map/dot_general | solution.py:89
  117.5 0.0 all-reduce.3.cloned.1.call-update
  117.5 0.0 all-gather.5.cloned.1.call-start
  117.6 21.7 %all-reduce.3.cloned.1.call-done = f32[64,1024]{1,0:T(8,128)} async-done(((f32[64,1024]{1,0:T(8,128)}), f32[64,1024]{1,0:T(8,128)}) %all-reduce.3.cloned.1.call-update) | async-done | bytes 262160 | tf_op jit(solution)/shard_map/psum | solution.py:92
  139.3 0.0 all-gather.5.cloned.1.call-update
  139.3 53.0 %all-gather.5.cloned.1.call-done = f32[1024,1024]{1,0:T(8,128)} async-done(((f32[64,1024]{1,0:T(8,128)}), f32[1024,1024]{1,0:T(8,128)}) %all-gather.5.cloned.1.call-update) | async-done | bytes 4194320 | tf_op jit(solution)/shard_map/all_gather | solution.py:93
  192.3 2.6 abs_reduce_fusion
  194.8 0.6 reduce_max.9
  195.4 11.7 %fusion.18 = f32[1024,1024]{1,0:T(8,128)S(1)} fusion(f32[1024,1024]{1,0:T(8,128)} %all-gather.5.cloned.1.call-done, f32[]{:T(128)} %reduce_max.9), kind=kOutput, calls=%fused_computation.24 | convolution fusion | flops 6443499520 | bytes 8388612 | tf_op jit(solution)/shard_map/dot_general | solution.py:33
  207.2 8.6 %add_convert_fusion = bf16[1024,1024]{1,0:T(8,128)(2,1)S(1)} fusion(f32[1024,1024]{1,0:T(8,128)S(1)} %fusion.18, f32[1024,1024]{1,0:T(8,128)S(1)} %copy-done, f32[]{:T(128)} %reduce_max.9), kind=kOutput, calls=%fused_computation.8 | convolution fusion | flops 6457131008 | bytes 10485764 | tf_op jit(solution)/shard_map/dot_general | solution.py:35
  215.8 19.5 %multiply_reduce_fusion = (f32[5632]{0:T(1024)S(1)}, f32[1024,5632]{1,0:T(8,128)}) fusion(bf16[1024,1024]{1,0:T(8,128)(2,1)S(1)} %add_convert_fusion, bf16[5632,1024]{1,0:T(8,128)(2,1)} %all-gather.3.cloned.1.call-done), kind=kOutput, calls=%fused_computation.1 | convolution fusion | flops 11822688256 | bytes 36722688 | tf_op jit(solution)/shard_map/dot_general | solution.py:24
  235.3 8.7 %multiply_convert_fusion = bf16[1024,5632]{1,0:T(8,128)(2,1)S(1)} fusion(f32[1024,5632]{1,0:T(8,128)} %get-tuple-element.8, f32[5632]{0:T(1024)S(1)} %add_rsqrt_fusion), kind=kLoop, calls=%fused_computation | loop fusion | flops 11534336 | bytes 34625536 | tf_op jit(solution)/shard_map/convert_element_type | solution.py:25
  244.0 7.7 %fusion.32 = (f32[352]{0:T(512)S(1)}, bf16[352,5632]{1,0:T(8,128)(2,1)}) fusion(bf16[1024,5632]{1,0:T(8,128)(2,1)S(1)} %multiply_convert_fusion, s32[]{:T(128)S(6)} %select_n.21, s32[5632]{0:T(1024)S(1)} %all-reduce, s32[352]{0:T(512)S(1)} %reduce.1), kind=kOutput, calls=%fused_computation.44 | convolution fusion | flops 4073963264 | bytes 16313732 | tf_op jit(solution)/shard_map/dot_general | solution.py:39
  251.7 6.5 %multiply_reduce_fusion.1 = (f32[352]{0:T(512)S(1)}, f32[352,1024]{1,0:T(8,128)S(1)}) fusion(f32[352]{0:T(512)S(1)} %compare_select_fusion, bf16[1024,5632]{1,0:T(8,128)(2,1)S(1)} %multiply_convert_fusion, bf16[352,5632]{1,0:T(8,128)(2,1)} %get-tuple-element.10), kind=kOutput, calls=%fused_computation.26 | convolution fusion | flops 4061167360 | bytes 16943872 | tf_op jit(solution)/shard_map/dot_general | solution.py:44
  258.2 1.1 multiply_convert_fusion.1
  (8 shorter events, 0.0 us)
Async XLA Ops:
  6.5 100.7 %all-gather.3.cloned.1.call-start = ((), (), s32[]{:S(2)}) async-start(), calls=%async_computation | async-start | bytes 12255232 | tf_op jit(solution)/shard_map/all_gather | solution.py:85
  7.3 132.0 %all-reduce.3.cloned.1.call-start = ((), (), s32[]{:S(2)}) async-start(), calls=%async_computation.1 | async-start | bytes 524288 | tf_op jit(solution)/shard_map/psum | solution.py:92
  117.5 74.8 %all-gather.5.cloned.1.call-start = ((), (), s32[]{:S(2)}) async-start(), calls=%async_computation.2 | async-start | bytes 4456448 | tf_op jit(solution)/shard_map/all_gather | solution.py:93
  195.4 11.7 %copy-start = (f32[1024,1024]{1,0:T(8,128)S(1)}, f32[1024,1024]{1,0:T(8,128)}, u32[]{:S(2)}) copy-start(f32[1024,1024]{1,0:T(8,128)} %all-gather.5.cloned.1.call-done) | copy-start | bytes 12582916
Sparse Core Ops, SparseCore 0:
  9.6 97.5 all-gather.2
  117.6 21.6 all-reduce.2
  141.7 50.5 all-gather.4
where the time goes:
time: 266 us
  waiting for transfers between devices  107 us (40%)
  blocking collectives  65.3 us (25%)
  matrix products  57.3 us (22%)
  other arithmetic  21.4 us (8%)
  between operations  13.8 us (5%)
    unnamed x1, blocking collectives  65.3 us
    all_gather x1, waiting for transfers between devices, by_gather(): moment = lax.all_gather(part, 'rows', axis=0, tiled=True)  53 us
    all_gather x1, waiting for transfers between devices, by_gather(): everyone = lax.all_gather(embeddings, 'rows', axis=0, tiled=True)  31.2 us
    psum x1, waiting for transfers between devices, by_gather(): part = lax.psum(part, 'rep')  21.7 us
    dot_general x1, matrix products, whiten(): mapped = jnp.dot(embedded, inverse_root, preferred_element_type=jnp.float32)  19.5 us
    dot_general x1, matrix products, root_of(): square = jnp.dot(y, y, precision=SPLIT)  11.7 us
    convert_element_type x1, other arithmetic, whiten(): (mapped * lax.rsqrt(jnp.mean(mapped * mapped, axis=1, keepdims=True) + EP...  8.69 us
    dot_general x1, matrix products, root_of(): jnp.dot(square, inner, precision=SPLIT)  8.6 us
  transfers between devices with their start and end apart: 3, of which 3 were waited for; matrix products, arithmetic and copies ran while one was open for 1% of the time, Pallas kernels for 0%

commit v1 on v0

--- a/solution.py
+++ b/solution.py
@@ -89,7 +89,7 @@
     part = lax.dot_general(
         own, masked, (((0,), (0,)), ((), ())), preferred_element_type=jnp.float32
     )
-    part = lax.psum(part, "rep")
+    part = jnp.sum(lax.all_gather(part, "rep"), axis=0)
     moment = lax.all_gather(part, "rows", axis=0, tiled=True)
     whitened = whiten(everyone, root_of(moment))
     mine = lax.dynamic_slice_in_dim(whitened, lax.axis_index("rows") * rows_here, rows_here, 0)

time: 266 us -> 250 us (0.940)
  waiting for transfers between devices: 107 us -> 81.1 us
  blocking collectives: 65.3 us -> 74.4 us
    psum x1 -> x0, waiting for transfers between devices: 21.7 us -> none  [by_gather(): part = lax.psum(part, 'rep')]
    all_gather x0 -> x1, blocking collectives: none -> 9.15 us  [by_gather(): part = jnp.sum(lax.all_gather(part, 'rep'), axis=0)]
    all_gather x1, waiting for transfers between devices: 53 us -> 49.1 us  [by_gather(): moment = lax.all_gather(part, 'rows', axis=0, tiled=True)]
  transfers between devices with their start and end apart: 3 -> 2, of which waited for: 3 -> 2; matrix products, arithmetic and copies ran while one was open for 1% -> 1% of each run, Pallas kernels for 0% -> 0%
where the time goes in v1:
time: 250 us
  waiting for transfers between devices  81.1 us (32%)
  blocking collectives  74.4 us (30%)
  matrix products  56.6 us (23%)
  other arithmetic  22.1 us (9%)
  between operations  14.1 us (6%)
    unnamed x1, blocking collectives  65.3 us
    all_gather x1, waiting for transfers between devices, by_gather(): moment = lax.all_gather(part, 'rows', axis=0, tiled=True)  49.1 us
    all_gather x1, waiting for transfers between devices, by_gather(): everyone = lax.all_gather(embeddings, 'rows', axis=0, tiled=True)  31.2 us
    dot_general x1, matrix products, whiten(): mapped = jnp.dot(embedded, inverse_root, preferred_element_type=jnp.float32)  19.5 us
    dot_general x1, matrix products, root_of(): square = jnp.dot(y, y, precision=SPLIT)  11.7 us
    all_gather x1, blocking collectives, by_gather(): part = jnp.sum(lax.all_gather(part, 'rep'), axis=0)  9.15 us
    convert_element_type x1, other arithmetic, whiten(): (mapped * lax.rsqrt(jnp.mean(mapped * mapped, axis=1, keepdims=True) + EP...  8.69 us
    dot_general x1, matrix products, root_of(): jnp.dot(square, inner, precision=SPLIT)  8.6 us
  transfers between devices with their start and end apart: 2, of which 2 were waited for; matrix products, arithmetic and copies ran while one was open for 1% of the time, Pallas kernels for 0%

profile of v1, /device:TPU:0, one launch (start us, length us, event | category | flops | bytes accessed | tf_op | source)
XLA Modules:
  0.0 249.6 jit_solution(2861297987380609151)
XLA Ops:
  6.5 0.0 all-gather.4.cloned.1.call-start
  6.5 0.7 all-gather.4.cloned.1.call-update
  7.3 0.0 all-gather.6.cloned.1.call-start
  7.3 0.7 reduce.1
  8.0 1.2 dynamic-slice.4
  9.9 0.7 fusion.31
  10.6 0.1 select_dynamic-update-slice_fusion
  10.7 65.3 %all-reduce = s32[5632]{0:T(1024)S(1)} all-reduce(s32[5632]{0:T(1024)S(1)} %select_dynamic-update-slice_fusion), channel_id=1, replica_groups=mesh['rows'=16,'rep'=2] {'rows'}, use_global_device_ids=true, to_apply=%add | all-reduce | flops 5632 | bytes 45056
  76.0 31.2 %all-gather.4.cloned.1.call-done = bf16[5632,1024]{1,0:T(8,128)(2,1)} async-done(((bf16[352,1024]{1,0:T(8,128)(2,1)}), bf16[5632,1024]{1,0:T(8,128)(2,1)}) %all-gather.4.cloned.1.call-update) | async-done | bytes 11534352 | tf_op jit(solution)/shard_map/all_gather | solution.py:85
  107.2 7.0 %broadcast_multiply_fusion = bf16[5632,1024]{1,0:T(8,128)(2,1)S(1)} fusion(bf16[5632,1024]{1,0:T(8,128)(2,1)} %all-gather.4.cloned.1.call-done, bf16[5632]{0:T(1024)(128)(2,1)S(1)} %compare_convert_fusion), kind=kLoop, calls=%fused_computation.7 | loop fusion | flops 5767168 | bytes 23079936 | tf_op jit(solution)/shard_map/mul | solution.py:87
  114.2 2.6 %fusion.19 = f32[64,1024]{1,0:T(8,128)S(1)} fusion(bf16[5632,1024]{1,0:T(8,128)(2,1)S(1)} %broadcast_multiply_fusion, s32[]{:T(128)S(6)} %select_n.20), kind=kOutput, calls=%fused_computation.27 | convolution fusion | flops 738197504 | bytes 13238276 | tf_op jit(solution)/shard_map/dot_general | solution.py:89
  116.8 9.1 %all-gather = f32[128,1024]{1,0:T(8,128)S(1)} all-gather(f32[64,1024]{1,0:T(8,128)S(1)} %fusion.19), channel_id=2, replica_groups=mesh['rows'=16,'rep'=2] {'rep'}, dimensions={0}, use_global_device_ids=true | all-gather | bytes 786432 | tf_op jit(solution)/shard_map/all_gather | solution.py:92
  125.9 0.7 reduce_sum.45
  126.7 0.0 all-gather.6.cloned.1.call-update
  126.7 49.1 %all-gather.6.cloned.1.call-done = f32[1024,1024]{1,0:T(8,128)} async-done(((f32[64,1024]{1,0:T(8,128)}), f32[1024,1024]{1,0:T(8,128)}) %all-gather.6.cloned.1.call-update) | async-done | bytes 4194320 | tf_op jit(solution)/shard_map/all_gather | solution.py:93
  175.8 2.6 %abs_reduce_fusion = f32[1024]{0:T(1024)S(1)} fusion(f32[1024,1024]{1,0:T(8,128)} %all-gather.6.cloned.1.call-done), kind=kLoop, calls=%fused_computation.15 | loop fusion | flops 2096128 | bytes 4198400 | tf_op jit(solution)/shard_map/reduce_sum | solution.py:31
  178.4 0.6 reduce_max.9
  179.0 11.7 %fusion.18 = f32[1024,1024]{1,0:T(8,128)S(1)} fusion(f32[1024,1024]{1,0:T(8,128)} %all-gather.6.cloned.1.call-done, f32[]{:T(128)} %reduce_max.9), kind=kOutput, calls=%fused_computation.24 | convolution fusion | flops 6443499520 | bytes 8388612 | tf_op jit(solution)/shard_map/dot_general | solution.py:33
  190.7 8.6 %add_convert_fusion = bf16[1024,1024]{1,0:T(8,128)(2,1)S(1)} fusion(f32[1024,1024]{1,0:T(8,128)S(1)} %fusion.18, f32[1024,1024]{1,0:T(8,128)S(1)} %copy-done, f32[]{:T(128)} %reduce_max.9), kind=kOutput, calls=%fused_computation.8 | convolution fusion | flops 6457131008 | bytes 10485764 | tf_op jit(solution)/shard_map/dot_general | solution.py:35
  199.3 19.5 %multiply_reduce_fusion = (f32[5632]{0:T(1024)S(1)}, f32[1024,5632]{1,0:T(8,128)}) fusion(bf16[1024,1024]{1,0:T(8,128)(2,1)S(1)} %add_convert_fusion, bf16[5632,1024]{1,0:T(8,128)(2,1)} %all-gather.4.cloned.1.call-done), kind=kOutput, calls=%fused_computation.1 | convolution fusion | flops 11822688256 | bytes 36722688 | tf_op jit(solution)/shard_map/dot_general | solution.py:24
  218.8 8.7 %multiply_convert_fusion = bf16[1024,5632]{1,0:T(8,128)(2,1)S(1)} fusion(f32[1024,5632]{1,0:T(8,128)} %get-tuple-element.8, f32[5632]{0:T(1024)S(1)} %add_rsqrt_fusion), kind=kLoop, calls=%fused_computation | loop fusion | flops 11534336 | bytes 34625536 | tf_op jit(solution)/shard_map/convert_element_type | solution.py:25
  227.5 7.7 %fusion.32 = (f32[352]{0:T(512)S(1)}, bf16[352,5632]{1,0:T(8,128)(2,1)}) fusion(bf16[1024,5632]{1,0:T(8,128)(2,1)S(1)} %multiply_convert_fusion, s32[]{:T(128)S(6)} %select_n.21, s32[5632]{0:T(1024)S(1)} %all-reduce, s32[352]{0:T(512)S(1)} %reduce.1), kind=kOutput, calls=%fused_computation.44 | convolution fusion | flops 4073963264 | bytes 16313732 | tf_op jit(solution)/shard_map/dot_general | solution.py:39
  235.2 6.5 %multiply_reduce_fusion.1 = (f32[352]{0:T(512)S(1)}, f32[352,1024]{1,0:T(8,128)S(1)}) fusion(f32[352]{0:T(512)S(1)} %compare_select_fusion, bf16[1024,5632]{1,0:T(8,128)(2,1)S(1)} %multiply_convert_fusion, bf16[352,5632]{1,0:T(8,128)(2,1)} %get-tuple-element.10), kind=kOutput, calls=%fused_computation.26 | convolution fusion | flops 4061167360 | bytes 16943872 | tf_op jit(solution)/shard_map/dot_general | solution.py:44
  241.7 1.1 multiply_convert_fusion.1
  (7 shorter events, 0.0 us)
Async XLA Ops:
  6.5 100.7 %all-gather.4.cloned.1.call-start = ((), (), s32[]{:S(2)}) async-start(), calls=%async_computation | async-start | bytes 12255232 | tf_op jit(solution)/shard_map/all_gather | solution.py:85
  7.3 168.6 %all-gather.6.cloned.1.call-start = ((), (), s32[]{:S(2)}) async-start(), calls=%async_computation.1 | async-start | bytes 4456448 | tf_op jit(solution)/shard_map/all_gather | solution.py:93
  179.0 11.7 %copy-start = (f32[1024,1024]{1,0:T(8,128)S(1)}, f32[1024,1024]{1,0:T(8,128)}, u32[]{:S(2)}) copy-start(f32[1024,1024]{1,0:T(8,128)} %all-gather.6.cloned.1.call-done) | copy-start | bytes 12582916
Sparse Core Ops, SparseCore 0:
  9.6 97.5 all-gather.3
  126.8 48.9 all-gather.5
